TPU v7x, 32 devices: a whole 2x2x4 slice. The times are simulated.
32 devices in a mesh: lat: 8 (over z, x), deg: 4 (over y, core).
Axes of the slice: x: 2, y: 2, z: 4, core: 2. Of those that a mesh axis runs over, the one named last changes fastest.
Arguments:
- eta_tl: float32 [64, 10752], P('lat'), may hold values from -6 to 6
- vel_tl: float32 [2, 64, 10752], P(None, 'lat'), may hold values from -6 to 6
- eta_adj: float32 [64, 10752], P('lat'), may hold values from -6 to 6
- vel_adj: float32 [2, 64, 10752], P(None, 'lat'), may hold values from -6 to 6
- depth: float32 [64, 10752], P('lat'), may hold values from 0.2 to 1
- drag: float32 [64, 10752], P('lat'), may hold values from 0.01 to 0.3
- ocean: int32 [64, 10752], P('lat'), may hold values 0 or 1
- basis: bfloat16 [1024, 64, 1024], P('lat', None, 'deg'), may hold values from -5 to 5
- love: float32 [1024], P('deg'), may hold values from 0.05 to 0.5
Outputs:
- eta_tl_out: float32 [64, 10752], P('lat')
- vel_tl_out: float32 [2, 64, 10752], P(None, 'lat')
- eta_adj_out: float32 [64, 10752], P('lat')
- vel_adj_out: float32 [2, 64, 10752], P(None, 'lat')
All inputs are finite; a program needn't handle non-finite values. No bound on the sum of `ocean` on one device may be relied on, other than what follows from the above.
Results may differ from a plain program's by a relative error of at most 0.02.
Values may be sent and summed in bfloat16 or wider, within the bound.
A program may use at most 320 MiB of HBM per device.

v0:
```python
import jax
import jax.numpy as jnp
from jax import lax
from jax.sharding import PartitionSpec as P

STEPS = 2
kappa_x = 0.3
kappa_y = 0.4


def as_sent(value):
    return jax.tree.map(lambda a: a.astype(jnp.bfloat16) if a.dtype == jnp.float32 else a, value)


def passed_along(value, axis, by):
    length = lax.axis_size(axis)
    pairs = [(i, i + by) for i in range(length) if 0 <= i + by < length]
    return lax.ppermute(value, axis, pairs)


def trig_table(orders, lon_count):
    lon_cells = jnp.arange(lon_count, dtype=jnp.int32)
    phase_index = lon_cells[:, None] * orders[None, :] % lon_count
    angles = phase_index.astype(jnp.float32) * (2.0 * jnp.pi / lon_count)
    return jnp.concatenate([jnp.cos(angles), jnp.sin(angles)], axis=1).astype(jnp.bfloat16)


def order_factor(orders):
    return jnp.where(orders == 0, 1.0, 2.0).astype(jnp.bfloat16)


def analyse(stacked, analysis_weight, table_now, order_count):
    row_count = stacked.shape[1]
    lon_count = stacked.shape[2]
    flat_rows = stacked.astype(jnp.bfloat16).reshape(2 * row_count, lon_count)
    spectra = lax.dot_general(
        table_now, flat_rows, (((0,), (1,)), ((), ())), preferred_element_type=jnp.float32
    )
    spectra = spectra.reshape(2, order_count, 2, row_count) * (1.0 / lon_count)
    return (spectra * analysis_weight[None, None, :, :]).astype(jnp.bfloat16)


def legendre(spectra, basis, love):
    coeffs = jnp.einsum("cmfi,mil->cmfl", spectra, basis, preferred_element_type=jnp.float32)
    scaled = (coeffs * love[None, None, None, :]).astype(jnp.bfloat16)
    return jnp.einsum("cmfl,mil->cmfi", scaled, basis, preferred_element_type=jnp.float32)


def synthesise(coeffs, factors, table_now, output_weight):
    order_count = coeffs.shape[1]
    row_count = coeffs.shape[3]
    scaled = (coeffs * factors[None, :, None, None]).reshape(2 * order_count, 2 * row_count)
    grid_out = lax.dot_general(
        scaled, table_now, (((0,), (1,)), ((), ())), preferred_element_type=jnp.float32
    )
    return grid_out.reshape(2, row_count, -1) * output_weight[:, :, None]


def from_north(edge_row):
    return passed_along(as_sent(edge_row), "lat", -1).astype(edge_row.dtype)


def from_south(edge_row):
    return passed_along(as_sent(edge_row), "lat", 1).astype(edge_row.dtype)


def on_device(eta_tl, vel_tl, eta_adj, vel_adj, depth, drag, ocean, basis, love):
    row_count = eta_tl.shape[0]
    lon_count = eta_tl.shape[1]
    lat_count = lax.axis_size("lat")
    total_rows = row_count * lat_count
    first_row = lax.axis_index("lat") * row_count
    indices = first_row + jnp.arange(row_count, dtype=jnp.int32)
    latitude = (indices.astype(jnp.float32) + 0.5) * (jnp.pi / total_rows) - 0.5 * jnp.pi
    cosine = jnp.cos(latitude)
    quad_weight = jnp.pi / total_rows * cosine
    east_factor = (kappa_x / (0.5 + 0.5 * cosine))[:, None]
    wet_mask = ocean.astype(jnp.float32)
    north_depth, north_wet = (
        passed_along(depth[:1].astype(jnp.bfloat16), "lat", -1).astype(jnp.float32),
        passed_along(wet_mask[:1].astype(jnp.bfloat16), "lat", -1).astype(jnp.float32),
    )
    depth_up = jnp.concatenate([depth[1:], north_depth], 0)
    wet_up = jnp.concatenate([wet_mask[1:], north_wet], 0)
    mask_u = wet_mask * jnp.roll(wet_mask, -1, 1)
    mask_v = wet_mask * wet_up
    depth_u = 0.5 * (depth + jnp.roll(depth, -1, 1))
    depth_v = 0.5 * (depth + depth_up)
    retain = 1.0 - drag
    ones_weight = jnp.ones_like(quad_weight)
    analysis_weight = jnp.stack([quad_weight, ones_weight])
    output_weight = jnp.stack([ones_weight, quad_weight])
    owned_count = basis.shape[0]
    order_total = owned_count * lat_count
    full_orders = jnp.arange(order_total, dtype=jnp.int32)
    full_table = trig_table(full_orders, lon_count)
    full_factor = order_factor(full_orders)
    state_eta, state_vel = (eta_tl, vel_tl)
    back_eta, back_vel = (eta_adj, vel_adj)
    for step_index in range(STEPS):
        flux_east = east_factor * wet_mask * back_eta
        flux_north = kappa_y * wet_mask * back_eta
        north_up = jnp.concatenate([flux_north[1:], from_north(flux_north[:1])], 0)
        p_term = mask_u * (back_vel[0] + depth_u * (jnp.roll(flux_east, -1, 1) - flux_east))
        q_term = mask_v * (back_vel[1] + depth_v * (north_up - flux_north))
        q_down = jnp.concatenate([from_south(q_term[-1:]), q_term[:-1]], 0)
        flux_p = east_factor * p_term
        psi_bar = flux_p - jnp.roll(flux_p, 1, 1) + kappa_y * (q_term - q_down)
        spectra = analyse(jnp.stack([state_eta, psi_bar]), analysis_weight, full_table, order_total)
        owned_rows = lax.all_to_all(spectra, "lat", split_axis=1, concat_axis=3, tiled=True)
        partial_value = legendre(owned_rows, basis, love)
        total_sum = lax.psum(partial_value.astype(jnp.bfloat16), "deg")
        banded = lax.all_to_all(total_sum, "lat", split_axis=3, concat_axis=1, tiled=True)
        loads = synthesise(banded, full_factor, full_table, output_weight)
        psi_now = state_eta - loads[0]
        psi_up = jnp.concatenate([psi_now[1:], from_north(psi_now[:1])], 0)
        new_u = mask_u * (
            retain * state_vel[0] - east_factor * (jnp.roll(psi_now, -1, 1) - psi_now)
        )
        new_v = mask_v * (retain * state_vel[1] - kappa_y * (psi_up - psi_now))
        flux_x = depth_u * new_u
        flux_y = depth_v * new_v
        flux_down = jnp.concatenate([from_south(flux_y[-1:]), flux_y[:-1]], 0)
        state_eta = state_eta - wet_mask * (
            east_factor * (flux_x - jnp.roll(flux_x, 1, 1)) + kappa_y * (flux_y - flux_down)
        )
        state_vel = jnp.stack([new_u, new_v])
        back_eta = back_eta + psi_bar - loads[1]
        back_vel = jnp.stack([retain * p_term, retain * q_term])
    return (state_eta, state_vel, back_eta, back_vel)


def solution(mesh):
    in_specs = (
        P("lat", None),
        P(None, "lat", None),
        P("lat", None),
        P(None, "lat", None),
        P("lat", None),
        P("lat", None),
        P("lat", None),
        P("lat", None, "deg"),
        P("deg"),
    )
    out_specs = (P("lat", None), P(None, "lat", None), P("lat", None), P(None, "lat", None))
    return jax.shard_map(
        on_device, mesh=mesh, in_specs=in_specs, out_specs=out_specs, check_vma=False
    )
```

profile of v0, /device:TPU:0, one launch (start us, length us, event | category | flops | bytes accessed | tf_op | source)
XLA Modules:
  0.0 552.0 jit_solution(11705418563088993422)
XLA Ops:
  7.3 1.2 multiply_multiply_fusion.3
  8.5 1.3 collective-permute-start.2
  9.8 1.0 slice.281
  10.8 1.3 collective-permute-start.1
  12.1 1.0 convert_element_type.110
  13.2 1.3 collective-permute-start
  14.5 187.3 %sine_convert_fusion = (bf16[10752,1024]{1,0:T(8,128)(2,1)}, bf16[10752,1024]{1,0:T(8,128)(2,1)}) fusion(), kind=kLoop, calls=%fused_computation.8 | loop fusion | flops 121110528 | bytes 44040192 | tf_op jit(solution)/shard_map/convert.19
  202.5 29.5 %fusion.9 = bf16[2048,10752]{0,1:T(8,128)(2,1)} fusion(bf16[10752,1024]{1,0:T(8,128)(2,1)} %get-tuple-element.48, bf16[10752,1024]{1,0:T(8,128)(2,1)} %get-tuple-element.49), kind=kLoop, calls=%fused_computation.14 | loop fusion | flops 88080384 | bytes 88080384 | tf_op jit(solution)/shard_map/dot_general | solution.py:36
  232.9 2.4 broadcast_multiply_fusion.1
  235.3 6.7 %collective-permute-start.3 = (bf16[1,10752]{1,0:T(2,128)(2,1)S(1)}, bf16[1,10752]{1,0:T(2,128)(2,1)S(1)}, u32[]{:S(2)}, u32[]{:S(2)}) collective-permute-start(bf16[1,10752]{1,0:T(2,128)(2,1)S(1)} %slice.279), channel_id=1, source_target_pairs={{0,4},{4,8},{8,12},{12,16},{16,20},{20,24},{24,28},{1,5},{5,9},{9,... | collective-permute-start | bytes 64520 | tf_op jit(solution)/shard_map/ppermute | solution.py:18
  242.1 56.8 %copy.41 = bf16[2048,10752]{1,0:T(8,128)(2,1)} copy(bf16[2048,10752]{0,1:T(8,128)(2,1)} %fusion.9) | data formatting | bytes 88080384 | tf_op jit(solution)/shard_map/dot_general | solution.py:36
  299.9 19.5 %fusion.66 = bf16[2,1024,2,8]{1,3,2,0:T(8,128)(2,1)S(1)} fusion(bf16[2,1024,10752,1]{2,1,3,0:T(8,128)(2,1)} %bitcast.190, bf16[1,8,10752]{2,1,0:T(8,128)(2,1)S(1)} %get-tuple-element.22, bf16[1,8,10752]{2,1,0:T(8,128)(2,1)S(1)} %copy-done.10, f32[2,8]{1,0:T(2,128)S(1)} %get-tuple-element.46), kind=kOutput, calls=%fused_computation.37 | convolution fusion | flops 705396736 | bytes 44449856 | tf_op jit(solution)/shard_map/dot_general | solution.py:36
  320.1 1.1 reshape.79
  321.2 14.8 %all_to_all.72 = bf16[8,2,2048]{2,1,0:T(2,128)(2,1)S(1)} all-to-all(bf16[8,2,2048]{2,1,0:T(2,128)(2,1)S(1)} %reshape.79), channel_id=1, replica_groups=mesh['lat'=8,'deg'=4] {'lat'}, dimensions={0} | all-to-all | bytes 131072 | tf_op jit(solution)/shard_map/all_to_all | solution.py:110
  336.0 1.2 reshape.80
  337.2 1.3 copy.59
  338.6 6.0 %fusion.61 = bf16[2,128,2,64]{3,2,0,1:T(2,128)(2,1)} fusion(bf16[128,64,256]{2,1,0:T(8,128)(2,1)} %param.16, bf16[2,128,2,64]{3,2,0,1:T(2,128)(2,1)S(1)} %copy.45, f32[256]{0:T(256)S(1)} %copy-done.11), kind=kOutput, calls=%fused_computation.34 | convolution fusion | flops 33849344 | bytes 4326400 | tf_op jit(solution)/shard_map/cmfl,mil->cmfi/dot_general | solution.py:46
  344.7 29.1 %all-reduce.5.cloned.1.call-done = bf16[2,128,2,64]{3,2,0,1:T(2,128)(2,1)} async-done(((bf16[2,128,2,64]{3,2,0,1:T(2,128)(2,1)}), bf16[2,128,2,64]{3,2,0,1:T(2,128)(2,1)}) %all-reduce.5.cloned.1.call-update) | async-done | bytes 65552 | tf_op jit(solution)/shard_map/psum | solution.py:112
  373.8 1.7 copy.46
  375.5 5.5 all-to-all-start.1
  381.1 6.8 %all-to-all-done.1 = bf16[2,128,2,64]{1,2,0,3:T(2,128)(2,1)S(1)} async-done(((bf16[2,128,2,64]{1,2,0,3:T(2,128)(2,1)}), bf16[2,128,2,64]{1,2,0,3:T(2,128)(2,1)S(1)}, u32[]{:S(2)}, u32[]{:S(2)}) %all-to-all-start.1) | async-done | bytes 65568 | tf_op jit(solution)/shard_map/all_to_all | solution.py:113
  388.0 18.4 %fusion.10 = f32[2,8,10752]{2,1,0:T(8,128)} fusion(bf16[10752,1024]{1,0:T(8,128)(2,1)} %get-tuple-element.48, bf16[10752,1024]{1,0:T(8,128)(2,1)} %get-tuple-element.49, f32[2,8]{1,0:T(2,128)S(1)} %get-tuple-element.47, bf16[2048,16]{0,1:T(8,128)(2,1)S(1)} %all_to_all.59, bf16[2048]{0:T(1024)(128)(2,1)S(1)} %bitcast.210), kind=kOutput, calls=%fused_computation.15 | convolution fusion | flops 792928256 | bytes 44798016 | tf_op jit(solution)/shard_map/dot_general | solution.py:53
  406.4 1.4 multiply_multiply_fusion
  407.8 1.3 collective-permute-start.4
  409.2 1.3 collective-permute-start.6
  410.7 3.0 collective-permute-done.4
  413.8 1.9 collective-permute-done.6
  415.8 2.4 fusion.139
  418.2 4.8 collective-permute-start.5
  423.2 2.3 collective-permute-start.7
  425.9 1.8 multiply_bitcast_fusion.1
  428.2 19.5 %fusion.67 = bf16[2,1024,2,8]{1,3,2,0:T(8,128)(2,1)S(1)} fusion(bf16[2,1024,10752,1]{2,1,3,0:T(8,128)(2,1)} %bitcast.191, bf16[1,8,10752]{2,1,0:T(8,128)(2,1)S(1)} %get-tuple-element.14, bf16[1,8,10752]{2,1,0:T(8,128)(2,1)S(1)} %get-tuple-element.12, f32[2,8]{1,0:T(2,128)S(1)} %get-tuple-element.46), kind=kOutput, calls=%fused_computation.38 | convolution fusion | flops 705396736 | bytes 44449856 | tf_op jit(solution)/shard_map/dot_general | solution.py:36
  448.4 1.1 reshape.81
  449.5 10.5 %all_to_all.73 = bf16[8,2,2048]{2,1,0:T(2,128)(2,1)S(1)} all-to-all(bf16[8,2,2048]{2,1,0:T(2,128)(2,1)S(1)} %reshape.81), channel_id=1, replica_groups=mesh['lat'=8,'deg'=4] {'lat'}, dimensions={0} | all-to-all | bytes 131072 | tf_op jit(solution)/shard_map/all_to_all | solution.py:110
  460.0 1.2 reshape.82
  461.2 1.3 copy.61
  463.3 6.1 %fusion.56 = bf16[2,128,2,64]{3,2,0,1:T(2,128)(2,1)} fusion(bf16[128,64,256]{2,1,0:T(8,128)(2,1)} %param.16, bf16[2,128,2,64]{3,2,0,1:T(2,128)(2,1)} %copy.52, f32[256]{0:T(256)S(1)} %copy-done.11), kind=kOutput, calls=%fused_computation.33 | convolution fusion | flops 33849344 | bytes 4326400 | tf_op jit(solution)/shard_map/cmfl,mil->cmfi/dot_general | solution.py:46
  469.4 28.1 %all-reduce.7.cloned.1.call-done = bf16[2,128,2,64]{3,2,0,1:T(2,128)(2,1)} async-done(((bf16[2,128,2,64]{3,2,0,1:T(2,128)(2,1)}), bf16[2,128,2,64]{3,2,0,1:T(2,128)(2,1)}) %all-reduce.7.cloned.1.call-update) | async-done | bytes 65552 | tf_op jit(solution)/shard_map/psum | solution.py:112
  497.6 1.0 copy.53
  498.6 12.2 %all_to_all.74 = bf16[2,128,2,64]{1,2,0,3:T(2,128)(2,1)S(1)} all-to-all(bf16[2,128,2,64]{1,2,0,3:T(2,128)(2,1)S(1)} %copy.53), channel_id=1, replica_groups=mesh['lat'=8,'deg'=4] {'lat'}, dimensions={3} | all-to-all | bytes 131072 | tf_op jit(solution)/shard_map/all_to_all | solution.py:113
  511.5 18.4 %fusion.13 = f32[2,8,10752]{2,1,0:T(8,128)} fusion(bf16[10752,1024]{1,0:T(8,128)(2,1)} %get-tuple-element.48, bf16[10752,1024]{1,0:T(8,128)(2,1)} %get-tuple-element.49, f32[2,8]{1,0:T(2,128)S(1)} %get-tuple-element.47, bf16[2048,16]{0,1:T(8,128)(2,1)} %all_to_all.67, bf16[2048]{0:T(1024)(128)(2,1)S(1)} %bitcast.211), kind=kOutput, calls=%fused_computation.16 | convolution fusion | flops 792928256 | bytes 44798016 | tf_op jit(solution)/shard_map/dot_general | solution.py:53
  529.9 1.9 fusion.68
  531.9 1.3 collective-permute-start.8
  533.2 1.9 pad_maximum_fusion.4
  535.2 2.5 collective-permute-done.8
  537.8 1.4 fusion.130
  539.3 3.2 collective-permute-start.9
  544.2 0.9 fusion.111
  (99 shorter events, 9.3 us)
Async XLA Ops:
  7.2 194.6 %copy-start.2 = (f32[8,10752]{1,0:T(8,128)S(1)}, f32[8,10752]{1,0:T(8,128)}, u32[]{:S(2)}) copy-start(f32[8,10752]{1,0:T(8,128)} %param.9) | copy-start | bytes 1032196
  7.2 366.7 %all-reduce.5.cloned.1.call-start = ((), (), s32[]{:S(2)}) async-start(), calls=%async_computation.4 | async-start | bytes 262144 | tf_op jit(solution)/shard_map/psum | solution.py:112
  8.5 224.2 %collective-permute-start.2 = (bf16[1,10752]{1,0:T(2,128)(2,1)S(1)}, bf16[1,10752]{1,0:T(2,128)(2,1)S(1)}, u32[]{:S(2)}, u32[]{:S(2)}) collective-permute-start(bf16[1,10752]{1,0:T(2,128)(2,1)S(1)} %slice.280), channel_id=1, source_target_pairs={{4,0},{8,4},{12,8},{16,12},{20,16},{24,20},{28,24},{5,1},{9,5},{13... | collective-permute-start | bytes 64520 | tf_op jit(solution)/shard_map/ppermute | solution.py:18
  10.8 221.9 %collective-permute-start.1 = (bf16[1,10752]{1,0:T(2,128)(2,1)S(1)}, bf16[1,10752]{1,0:T(2,128)(2,1)S(1)}, u32[]{:S(2)}, u32[]{:S(2)}) collective-permute-start(bf16[1,10752]{1,0:T(2,128)(2,1)S(1)} %slice.281), channel_id=1, source_target_pairs={{4,0},{8,4},{12,8},{16,12},{20,16},{24,20},{28,24},{5,1},{9,5},{13... | collective-permute-start | bytes 64520 | tf_op jit(solution)/shard_map/ppermute | solution.py:18
  13.2 219.7 %collective-permute-start = (bf16[1,10752]{1,0:T(2,128)(2,1)S(1)}, bf16[1,10752]{1,0:T(2,128)(2,1)S(1)}, u32[]{:S(2)}, u32[]{:S(2)}) collective-permute-start(bf16[1,10752]{1,0:T(2,128)(2,1)S(1)} %slice.282), channel_id=1, source_target_pairs={{4,0},{8,4},{12,8},{16,12},{20,16},{24,20},{28,24},{5,1},{9,5},{13... | collective-permute-start | bytes 64520 | tf_op jit(solution)/shard_map/ppermute | solution.py:18
  202.5 29.9 %copy-start.1 = (f32[8,10752]{1,0:T(8,128)S(1)}, f32[8,10752]{1,0:T(8,128)}, u32[]{:S(2)}) copy-start(f32[8,10752]{1,0:T(8,128)} %param.13) | copy-start | bytes 1032196
  202.5 30.4 %copy-start = (s32[8,10752]{1,0:T(8,128)S(1)}, s32[8,10752]{1,0:T(8,128)}, u32[]{:S(2)}) copy-start(s32[8,10752]{1,0:T(8,128)} %param.15) | copy-start | bytes 1032196
  202.5 30.4 %slice-start = ((f32[8,10752]{1,0:T(8,128)}), f32[8,1]{1,0:T(8,128)S(1)}, s32[]{:S(2)}) async-start(f32[8,10752]{1,0:T(8,128)} %param.13), calls=%async_computation.6 | async-start | bytes 8192 | tf_op jit(solution)/shard_map/jit(_roll_static)/slice | solution.py:87
  235.2 180.5 %copy-start.5 = (f32[8,10752]{1,0:T(8,128)}, f32[8,10752]{1,0:T(8,128)S(1)}, u32[]{:S(2)}) copy-start(f32[8,10752]{1,0:T(8,128)S(1)} %get-tuple-element.34) | copy-start | bytes 1032196
  235.3 63.6 %collective-permute-start.3 = (bf16[1,10752]{1,0:T(2,128)(2,1)S(1)}, bf16[1,10752]{1,0:T(2,128)(2,1)S(1)}, u32[]{:S(2)}, u32[]{:S(2)}) collective-permute-start(bf16[1,10752]{1,0:T(2,128)(2,1)S(1)} %slice.279), channel_id=1, source_target_pairs={{0,4},{4,8},{8,12},{12,16},{16,20},{20,24},{24,28},{1,5},{5,9},{9,... | collective-permute-start | bytes 64520 | tf_op jit(solution)/shard_map/ppermute | solution.py:18
  242.0 57.8 %copy-start.10 = (bf16[1,8,10752]{2,1,0:T(8,128)(2,1)S(1)}, bf16[1,8,10752]{2,1,0:T(8,128)(2,1)}, u32[]{:S(2)}) copy-start(bf16[1,8,10752]{2,1,0:T(8,128)(2,1)} %convert_bitcast_fusion.3) | copy-start | bytes 516100
  298.8 39.8 %copy-start.11 = (f32[256]{0:T(256)S(1)}, f32[256]{0:T(256)}, u32[]{:S(2)}) copy-start(f32[256]{0:T(256)} %param.17) | copy-start | bytes 3076
  338.6 77.2 %copy-start.3 = (f32[8,10752]{1,0:T(8,128)S(1)}, f32[8,10752]{1,0:T(8,128)}, u32[]{:S(2)}) copy-start(f32[8,10752]{1,0:T(8,128)} %param.14) | copy-start | bytes 1032196
  338.6 77.2 %copy-start.7 = (f32[8,10752]{1,0:T(8,128)S(1)}, f32[8,10752]{1,0:T(8,128)}, u32[]{:S(2)}) copy-start(f32[8,10752]{1,0:T(8,128)} %get-tuple-element.35) | copy-start | bytes 1032196
  375.5 12.4 %all-to-all-start.1 = ((bf16[2,128,2,64]{1,2,0,3:T(2,128)(2,1)}), bf16[2,128,2,64]{1,2,0,3:T(2,128)(2,1)S(1)}, u32[]{:S(2)}, u32[]{:S(2)}) async-start(bf16[2,128,2,64]{1,2,0,3:T(2,128)(2,1)} %copy.46), calls=%async_computation.1 | async-start | bytes 131072 | tf_op jit(solution)/shard_map/all_to_all | solution.py:113
  381.0 116.6 %all-reduce.7.cloned.1.call-start = ((), (), s32[]{:S(2)}) async-start(), calls=%async_computation.5 | async-start | bytes 262144 | tf_op jit(solution)/shard_map/psum | solution.py:112
  407.8 5.9 %collective-permute-start.4 = (bf16[1,10752]{1,0:T(2,128)(2,1)S(1)}, bf16[1,10752]{1,0:T(2,128)(2,1)S(1)}, u32[]{:S(2)}, u32[]{:S(2)}) collective-permute-start(bf16[1,10752]{1,0:T(2,128)(2,1)S(1)} %slice.278), channel_id=1, source_target_pairs={{4,0},{8,4},{12,8},{16,12},{20,16},{24,20},{28,24},{5,1},{9,5},{13... | collective-permute-start | bytes 64520 | tf_op jit(solution)/shard_map/ppermute | solution.py:18
  409.2 6.5 %collective-permute-start.6 = (bf16[1,10752]{1,0:T(2,128)(2,1)S(1)}, bf16[1,10752]{1,0:T(2,128)(2,1)S(1)}, u32[]{:S(2)}, u32[]{:S(2)}) collective-permute-start(bf16[1,10752]{1,0:T(2,128)(2,1)S(1)} %slice.276), channel_id=1, source_target_pairs={{4,0},{8,4},{12,8},{16,12},{20,16},{24,20},{28,24},{5,1},{9,5},{13... | collective-permute-start | bytes 64520 | tf_op jit(solution)/shard_map/ppermute | solution.py:18
  418.2 7.3 %collective-permute-start.5 = (bf16[1,10752]{1,0:T(2,128)(2,1)S(1)}, bf16[1,10752]{1,0:T(2,128)(2,1)S(1)}, u32[]{:S(2)}, u32[]{:S(2)}) collective-permute-start(bf16[1,10752]{1,0:T(2,128)(2,1)S(1)} %slice.277), channel_id=1, source_target_pairs={{0,4},{4,8},{8,12},{12,16},{16,20},{20,24},{24,28},{1,5},{5,9},{9,... | collective-permute-start | bytes 64520 | tf_op jit(solution)/shard_map/ppermute | solution.py:18
  423.2 4.8 collective-permute-start.7
  460.0 73.2 %copy-start.9 = (f32[1,8,10752]{2,1,0:T(8,128)S(1)}, f32[1,8,10752]{2,1,0:T(8,128)}, u32[]{:S(2)}) copy-start(f32[1,8,10752]{2,1,0:T(8,128)} %get-tuple-element.4) | copy-start | bytes 1032196
  463.3 74.5 %copy-start.4 = (f32[8,10752]{1,0:T(8,128)S(1)}, f32[8,10752]{1,0:T(8,128)}, u32[]{:S(2)}) copy-start(f32[8,10752]{1,0:T(8,128)} %param.14) | copy-start | bytes 1032196
  463.3 74.5 %copy-start.6 = (f32[8,10752]{1,0:T(8,128)S(1)}, f32[8,10752]{1,0:T(8,128)}, u32[]{:S(2)}) copy-start(f32[8,10752]{1,0:T(8,128)} %copy-done.5) | copy-start | bytes 1032196
  463.3 74.5 %copy-start.8 = (f32[8,10752]{1,0:T(8,128)S(1)}, f32[8,10752]{1,0:T(8,128)}, u32[]{:S(2)}) copy-start(f32[8,10752]{1,0:T(8,128)} %get-tuple-element.35) | copy-start | bytes 1032196
  531.9 5.9 %collective-permute-start.8 = (bf16[1,10752]{1,0:T(2,128)(2,1)S(1)}, bf16[1,10752]{1,0:T(2,128)(2,1)S(1)}, u32[]{:S(2)}, u32[]{:S(2)}) collective-permute-start(bf16[1,10752]{1,0:T(2,128)(2,1)S(1)} %slice.274), channel_id=1, source_target_pairs={{4,0},{8,4},{12,8},{16,12},{20,16},{24,20},{28,24},{5,1},{9,5},{13... | collective-permute-start | bytes 64520 | tf_op jit(solution)/shard_map/ppermute | solution.py:18
  539.3 4.9 collective-permute-start.9
Sparse Core Ops, SparseCore 0:
  344.8 28.9 all-reduce.4
  469.6 27.9 all-reduce.6
where the time goes:
time: 554 us; the launch traced here: 552 us
  other arithmetic  237 us (43%)
  matrix products  88 us (16%)
  local copies, waits for them, and re-layouts  72.5 us (13%)
  waiting for transfers between devices  72.3 us (13%)
  blocking collectives  37.5 us (7%)
  starting transfers between devices  30.4 us (5%)
  between operations  14.7 us (3%)
    another operation x1, other arithmetic  187 us
    psum x2, waiting for transfers between devices, on_device(): total_sum = lax.psum(partial_value.astype(jnp.bfloat16), 'deg')  57.2 us
    dot_general x1, local copies, waits for them, and re-layouts, analyse(): lax.dot_general(table_now, flat_rows, (((0,), (1,)), ((), ())), preferred...  56.8 us
    dot_general x2, matrix products, analyse(): lax.dot_general(table_now, flat_rows, (((0,), (1,)), ((), ())), preferred...  39 us
    dot_general x2, matrix products, synthesise(): lax.dot_general(scaled, table_now, (((0,), (1,)), ((), ())), preferred_el...  36.8 us
    dot_general x1, other arithmetic, analyse(): lax.dot_general(table_now, flat_rows, (((0,), (1,)), ((), ())), preferred...  29.5 us
    all_to_all x2, blocking collectives, on_device(): lax.all_to_all(spectra, 'lat', split_axis=1, concat_axis=3, tiled=True)  25.3 us
    ppermute x10, starting transfers between devices, passed_along(): return lax.ppermute(value, axis, pairs)  24.8 us
  transfers between devices with their start and end apart: 13, of which 7 were waited for; matrix products, arithmetic and copies ran while one was open for 51% of the time, Pallas kernels for 0%

commit v1 on v0

--- a/solution.py
+++ b/solution.py
@@ -109,7 +109,9 @@
         spectra = analyse(jnp.stack([state_eta, psi_bar]), analysis_weight, full_table, order_total)
         owned_rows = lax.all_to_all(spectra, "lat", split_axis=1, concat_axis=3, tiled=True)
         partial_value = legendre(owned_rows, basis, love)
-        total_sum = lax.psum(partial_value.astype(jnp.bfloat16), "deg")
+        total_sum = jnp.sum(
+            lax.all_gather(partial_value.astype(jnp.bfloat16), axis_name="deg"), axis=0
+        )
         banded = lax.all_to_all(total_sum, "lat", split_axis=3, concat_axis=1, tiled=True)
         loads = synthesise(banded, full_factor, full_table, output_weight)
         psi_now = state_eta - loads[0]

time: 554 us -> 491 us (0.89)
  waiting for transfers between devices: 72.3 us -> 21.9 us
  between operations: 14.7 us -> 1.29 us
  starting transfers between devices: 30.4 us -> 36.5 us
  local copies, waits for them, and re-layouts: 72.5 us -> 66.8 us
    psum x2 -> x0, waiting for transfers between devices: 57.2 us -> none  [on_device(): total_sum = lax.psum(partial_value.astype(jnp.bfloat16), 'deg')]
    all_to_all x2 -> x1, blocking collectives: 25.3 us -> 10.3 us  [on_device(): lax.all_to_all(spectra, 'lat', split_axis=1, concat_axis=3, tiled=True)]
    all_gather x0 -> x2, blocking collectives: none -> 15 us  [on_device(): lax.all_gather(partial_value.astype(jnp.bfloat16), axis_name='deg')]
    all_to_all x0 -> x1, starting transfers between devices: none -> 8.1 us  [on_device(): lax.all_to_all(spectra, 'lat', split_axis=1, concat_axis=3, tiled=True)]
    all_to_all x0 -> x1, waiting for transfers between devices: none -> 6.9 us  [on_device(): lax.all_to_all(spectra, 'lat', split_axis=1, concat_axis=3, tiled=True)]
  transfers between devices with their start and end apart: 13 -> 12, of which waited for: 7 -> 6; matrix products, arithmetic and copies ran while one was open for 51% -> 57% of each run, Pallas kernels for 0% -> 0%
where the time goes in v1:
time: 491 us; the launch traced here: 489 us
  other arithmetic  240 us (49%)
  matrix products  87.3 us (18%)
  local copies, waits for them, and re-layouts  66.8 us (14%)
  starting transfers between devices  36.5 us (7%)
  blocking collectives  34.6 us (7%)
  waiting for transfers between devices  21.9 us (4%)
    another operation x1, other arithmetic  187 us
    dot_general x1, local copies, waits for them, and re-layouts, analyse(): lax.dot_general(table_now, flat_rows, (((0,), (1,)), ((), ())), preferred...  51.4 us
    dot_general x2, matrix products, analyse(): lax.dot_general(table_now, flat_rows, (((0,), (1,)), ((), ())), preferred...  39 us
    dot_general x2, matrix products, synthesise(): lax.dot_general(scaled, table_now, (((0,), (1,)), ((), ())), preferred_el...  36.8 us
    dot_general x1, other arithmetic, analyse(): lax.dot_general(table_now, flat_rows, (((0,), (1,)), ((), ())), preferred...  29.5 us
    ppermute x10, starting transfers between devices, passed_along(): return lax.ppermute(value, axis, pairs)  25 us
    all_gather x2, blocking collectives, on_device(): lax.all_gather(partial_value.astype(jnp.bfloat16), axis_name='deg')  15 us
    dot_general x2, matrix products, legendre(): jnp.einsum('cmfl,mil->cmfi', scaled, basis, preferred_element_type=jnp.fl...  11.5 us
  transfers between devices with their start and end apart: 12, of which 6 were waited for; matrix products, arithmetic and copies ran while one was open for 57% of the time, Pallas kernels for 0%

profile of v1, /device:TPU:0, one launch (start us, length us, event | category | flops | bytes accessed | tf_op | source)
XLA Modules:
  0.0 488.7 jit_solution(7443802094811250249)
XLA Ops:
  0.7 1.2 multiply_multiply_fusion.3
  2.0 1.3 collective-permute-start.2
  3.3 1.0 slice.281
  4.3 1.3 collective-permute-start.1
  6.6 1.3 collective-permute-start
  7.9 187.3 %sine_convert_fusion = (bf16[10752,1024]{1,0:T(8,128)(2,1)}, bf16[10752,1024]{1,0:T(8,128)(2,1)}) fusion(), kind=kLoop, calls=%fused_computation.8 | loop fusion | flops 121110528 | bytes 44040192 | tf_op jit(solution)/shard_map/convert.21
  196.0 29.5 %fusion.9 = bf16[2048,10752]{0,1:T(8,128)(2,1)} fusion(bf16[10752,1024]{1,0:T(8,128)(2,1)} %get-tuple-element.48, bf16[10752,1024]{1,0:T(8,128)(2,1)} %get-tuple-element.49), kind=kLoop, calls=%fused_computation.14 | loop fusion | flops 88080384 | bytes 88080384 | tf_op jit(solution)/shard_map/dot_general | solution.py:36
  226.3 2.4 broadcast_multiply_fusion.1
  228.7 6.7 %collective-permute-start.3 = (bf16[1,10752]{1,0:T(2,128)(2,1)S(1)}, bf16[1,10752]{1,0:T(2,128)(2,1)S(1)}, u32[]{:S(2)}, u32[]{:S(2)}) collective-permute-start(bf16[1,10752]{1,0:T(2,128)(2,1)S(1)} %slice.279), channel_id=1, source_target_pairs={{0,4},{4,8},{8,12},{12,16},{16,20},{20,24},{24,28},{1,5},{5,9},{9,... | collective-permute-start | bytes 64520 | tf_op jit(solution)/shard_map/ppermute | solution.py:18
  235.5 51.4 %copy.28 = bf16[2048,10752]{1,0:T(8,128)(2,1)} copy(bf16[2048,10752]{0,1:T(8,128)(2,1)} %fusion.9) | data formatting | bytes 88080384 | tf_op jit(solution)/shard_map/dot_general | solution.py:36
  287.9 19.5 %fusion.66 = bf16[2,1024,2,8]{1,3,2,0:T(8,128)(2,1)S(1)} fusion(bf16[2,1024,10752,1]{2,1,3,0:T(8,128)(2,1)} %bitcast.190, bf16[1,8,10752]{2,1,0:T(8,128)(2,1)S(1)} %get-tuple-element.22, bf16[1,8,10752]{2,1,0:T(8,128)(2,1)S(1)} %copy-done.11, f32[2,8]{1,0:T(2,128)S(1)} %get-tuple-element.46), kind=kOutput, calls=%fused_computation.37 | convolution fusion | flops 705396736 | bytes 44449856 | tf_op jit(solution)/shard_map/dot_general | solution.py:36
  308.1 1.7 reshape.81
  309.8 8.1 %all-to-all-start = ((bf16[8,2,2048]{2,1,0:T(2,128)(2,1)}), bf16[8,2,2048]{2,1,0:T(2,128)(2,1)S(1)}, u32[]{:S(2)}, u32[]{:S(2)}) async-start(bf16[8,2,2048]{2,1,0:T(2,128)(2,1)} %reshape.81), calls=%async_computation | async-start | bytes 131072 | tf_op jit(solution)/shard_map/all_to_all | solution.py:110
  317.9 6.9 %all-to-all-done = bf16[8,2,2048]{2,1,0:T(2,128)(2,1)S(1)} async-done(((bf16[8,2,2048]{2,1,0:T(2,128)(2,1)}), bf16[8,2,2048]{2,1,0:T(2,128)(2,1)S(1)}, u32[]{:S(2)}, u32[]{:S(2)}) %all-to-all-start) | async-done | bytes 65568 | tf_op jit(solution)/shard_map/all_to_all | solution.py:110
  324.8 1.2 reshape.82
  326.0 1.3 copy.44
  327.5 5.4 %fusion.61 = bf16[2,128,2,64]{3,2,0,1:T(2,128)(2,1)S(1)} fusion(bf16[128,64,256]{2,1,0:T(8,128)(2,1)} %param.16, bf16[2,128,2,64]{3,2,0,1:T(2,128)(2,1)S(1)} %copy.32, f32[256]{0:T(256)S(1)} %copy-done.12), kind=kOutput, calls=%fused_computation.34 | convolution fusion | flops 33849344 | bytes 4326400 | tf_op jit(solution)/shard_map/cmfl,mil->cmfi/dot_general | solution.py:46
  332.9 7.3 %all-gather = bf16[8,128,2,64]{3,2,0,1:T(2,128)(2,1)S(1)} all-gather(bf16[2,128,2,64]{3,2,0,1:T(2,128)(2,1)S(1)} %fusion.61), channel_id=2, replica_groups=mesh['lat'=8,'deg'=4] {'deg'}, dimensions={0}, use_global_device_ids=true | all-gather | bytes 327680 | tf_op jit(solution)/shard_map/all_gather | solution.py:113
  340.2 1.2 reduce_sum.24
  342.1 3.4 all-to-all-start.1
  345.5 6.8 %all-to-all-done.1 = bf16[2,128,2,64]{1,0,2,3:T(2,128)(2,1)S(1)} async-done(((bf16[2,128,2,64]{1,0,2,3:T(2,128)(2,1)}), bf16[2,128,2,64]{1,0,2,3:T(2,128)(2,1)S(1)}, u32[]{:S(2)}, u32[]{:S(2)}) %all-to-all-start.1) | async-done | bytes 65568 | tf_op jit(solution)/shard_map/all_to_all | solution.py:115
  352.4 18.4 %fusion.10 = f32[2,8,10752]{2,1,0:T(8,128)} fusion(bf16[10752,1024]{1,0:T(8,128)(2,1)} %get-tuple-element.48, bf16[10752,1024]{1,0:T(8,128)(2,1)} %get-tuple-element.49, f32[2,8]{1,0:T(2,128)S(1)} %get-tuple-element.47, bf16[2048,16]{0,1:T(8,128)(2,1)S(1)} %all_to_all.59, bf16[2048]{0:T(1024)(128)(2,1)S(1)} %bitcast.214), kind=kOutput, calls=%fused_computation.15 | convolution fusion | flops 792928256 | bytes 44798016 | tf_op jit(solution)/shard_map/dot_general | solution.py:53
  370.9 1.3 multiply_multiply_fusion
  372.2 1.3 collective-permute-start.4
  373.5 1.3 collective-permute-start.6
  375.1 3.3 collective-permute-done.4
  378.4 1.6 collective-permute-done.6
  380.1 2.4 fusion.139
  382.6 4.8 collective-permute-start.5
  387.5 2.5 collective-permute-start.7
  390.5 1.8 multiply_bitcast_fusion.1
  392.8 19.5 %fusion.67 = bf16[2,1024,2,8]{1,3,2,0:T(8,128)(2,1)S(1)} fusion(bf16[2,1024,10752,1]{2,1,3,0:T(8,128)(2,1)} %bitcast.191, bf16[1,8,10752]{2,1,0:T(8,128)(2,1)S(1)} %get-tuple-element.14, bf16[1,8,10752]{2,1,0:T(8,128)(2,1)S(1)} %get-tuple-element.12, f32[2,8]{1,0:T(2,128)S(1)} %get-tuple-element.46), kind=kOutput, calls=%fused_computation.38 | convolution fusion | flops 705396736 | bytes 44449856 | tf_op jit(solution)/shard_map/dot_general | solution.py:36
  413.0 1.1 reshape.83
  414.1 10.3 %all_to_all.72 = bf16[8,2,2048]{2,1,0:T(2,128)(2,1)S(1)} all-to-all(bf16[8,2,2048]{2,1,0:T(2,128)(2,1)S(1)} %reshape.83), channel_id=1, replica_groups=mesh['lat'=8,'deg'=4] {'lat'}, dimensions={0} | all-to-all | bytes 131072 | tf_op jit(solution)/shard_map/all_to_all | solution.py:110
  424.3 1.2 reshape.84
  425.6 1.3 copy.46
  427.7 6.1 %fusion.56 = bf16[2,128,2,64]{3,2,0,1:T(2,128)(2,1)} fusion(bf16[128,64,256]{2,1,0:T(8,128)(2,1)} %param.16, bf16[2,128,2,64]{3,2,0,1:T(2,128)(2,1)} %copy.38, f32[256]{0:T(256)S(1)} %copy-done.12), kind=kOutput, calls=%fused_computation.33 | convolution fusion | flops 33849344 | bytes 4326400 | tf_op jit(solution)/shard_map/cmfl,mil->cmfi/dot_general | solution.py:46
  433.8 7.7 %all-gather.1 = bf16[8,128,2,64]{3,2,0,1:T(2,128)(2,1)} all-gather(bf16[2,128,2,64]{3,2,0,1:T(2,128)(2,1)} %fusion.56), channel_id=3, replica_groups=mesh['lat'=8,'deg'=4] {'deg'}, dimensions={0}, use_global_device_ids=true | all-gather | bytes 327680 | tf_op jit(solution)/shard_map/all_gather | solution.py:113
  441.5 2.6 reduce_sum.25
  444.0 1.0 copy.39
  445.1 9.3 %all_to_all.73 = bf16[2,128,2,64]{1,0,2,3:T(2,128)(2,1)S(1)} all-to-all(bf16[2,128,2,64]{1,0,2,3:T(2,128)(2,1)S(1)} %copy.39), channel_id=1, replica_groups=mesh['lat'=8,'deg'=4] {'lat'}, dimensions={3} | all-to-all | bytes 131072 | tf_op jit(solution)/shard_map/all_to_all | solution.py:115
  455.1 18.4 %fusion.13 = f32[2,8,10752]{2,1,0:T(8,128)} fusion(bf16[10752,1024]{1,0:T(8,128)(2,1)} %get-tuple-element.48, bf16[10752,1024]{1,0:T(8,128)(2,1)} %get-tuple-element.49, f32[2,8]{1,0:T(2,128)S(1)} %get-tuple-element.47, bf16[2048,16]{0,1:T(8,128)(2,1)} %all_to_all.67, bf16[2048]{0:T(1024)(128)(2,1)S(1)} %bitcast.215), kind=kOutput, calls=%fused_computation.16 | convolution fusion | flops 792928256 | bytes 44798016 | tf_op jit(solution)/shard_map/dot_general | solution.py:53
  473.5 1.9 fusion.68
  475.4 1.3 collective-permute-start.8
  476.7 1.9 pad_maximum_fusion.4
  478.8 2.5 collective-permute-done.8
  481.4 1.4 fusion.130
  482.8 3.2 collective-permute-start.9
  (98 shorter events, 11.9 us)
Async XLA Ops:
  0.6 194.6 %copy-start.2 = (f32[8,10752]{1,0:T(8,128)S(1)}, f32[8,10752]{1,0:T(8,128)}, u32[]{:S(2)}) copy-start(f32[8,10752]{1,0:T(8,128)} %param.9) | copy-start | bytes 1032196
  2.0 224.2 %collective-permute-start.2 = (bf16[1,10752]{1,0:T(2,128)(2,1)S(1)}, bf16[1,10752]{1,0:T(2,128)(2,1)S(1)}, u32[]{:S(2)}, u32[]{:S(2)}) collective-permute-start(bf16[1,10752]{1,0:T(2,128)(2,1)S(1)} %slice.280), channel_id=1, source_target_pairs={{4,0},{8,4},{12,8},{16,12},{20,16},{24,20},{28,24},{5,1},{9,5},{13... | collective-permute-start | bytes 64520 | tf_op jit(solution)/shard_map/ppermute | solution.py:18
  4.3 221.9 %collective-permute-start.1 = (bf16[1,10752]{1,0:T(2,128)(2,1)S(1)}, bf16[1,10752]{1,0:T(2,128)(2,1)S(1)}, u32[]{:S(2)}, u32[]{:S(2)}) collective-permute-start(bf16[1,10752]{1,0:T(2,128)(2,1)S(1)} %slice.281), channel_id=1, source_target_pairs={{4,0},{8,4},{12,8},{16,12},{20,16},{24,20},{28,24},{5,1},{9,5},{13... | collective-permute-start | bytes 64520 | tf_op jit(solution)/shard_map/ppermute | solution.py:18
  6.6 219.7 %collective-permute-start = (bf16[1,10752]{1,0:T(2,128)(2,1)S(1)}, bf16[1,10752]{1,0:T(2,128)(2,1)S(1)}, u32[]{:S(2)}, u32[]{:S(2)}) collective-permute-start(bf16[1,10752]{1,0:T(2,128)(2,1)S(1)} %slice.282), channel_id=1, source_target_pairs={{4,0},{8,4},{12,8},{16,12},{20,16},{24,20},{28,24},{5,1},{9,5},{13... | collective-permute-start | bytes 64520 | tf_op jit(solution)/shard_map/ppermute | solution.py:18
  195.9 29.9 %copy-start.1 = (f32[8,10752]{1,0:T(8,128)S(1)}, f32[8,10752]{1,0:T(8,128)}, u32[]{:S(2)}) copy-start(f32[8,10752]{1,0:T(8,128)} %param.13) | copy-start | bytes 1032196
  195.9 30.4 %copy-start = (s32[8,10752]{1,0:T(8,128)S(1)}, s32[8,10752]{1,0:T(8,128)}, u32[]{:S(2)}) copy-start(s32[8,10752]{1,0:T(8,128)} %param.15) | copy-start | bytes 1032196
  195.9 30.4 %slice-start = ((f32[8,10752]{1,0:T(8,128)}), f32[8,1]{1,0:T(8,128)S(1)}, s32[]{:S(2)}) async-start(f32[8,10752]{1,0:T(8,128)} %param.13), calls=%async_computation.4 | async-start | bytes 8192 | tf_op jit(solution)/shard_map/jit(_roll_static)/slice | solution.py:87
  228.7 151.4 %copy-start.5 = (f32[8,10752]{1,0:T(8,128)}, f32[8,10752]{1,0:T(8,128)S(1)}, u32[]{:S(2)}) copy-start(f32[8,10752]{1,0:T(8,128)S(1)} %get-tuple-element.34) | copy-start | bytes 1032196
  228.7 58.2 %collective-permute-start.3 = (bf16[1,10752]{1,0:T(2,128)(2,1)S(1)}, bf16[1,10752]{1,0:T(2,128)(2,1)S(1)}, u32[]{:S(2)}, u32[]{:S(2)}) collective-permute-start(bf16[1,10752]{1,0:T(2,128)(2,1)S(1)} %slice.279), channel_id=1, source_target_pairs={{0,4},{4,8},{8,12},{12,16},{16,20},{20,24},{24,28},{1,5},{5,9},{9,... | collective-permute-start | bytes 64520 | tf_op jit(solution)/shard_map/ppermute | solution.py:18
  235.5 52.4 %copy-start.11 = (bf16[1,8,10752]{2,1,0:T(8,128)(2,1)S(1)}, bf16[1,8,10752]{2,1,0:T(8,128)(2,1)}, u32[]{:S(2)}) copy-start(bf16[1,8,10752]{2,1,0:T(8,128)(2,1)} %convert_bitcast_fusion.3) | copy-start | bytes 516100
  286.9 40.6 %copy-start.12 = (f32[256]{0:T(256)S(1)}, f32[256]{0:T(256)}, u32[]{:S(2)}) copy-start(f32[256]{0:T(256)} %param.17) | copy-start | bytes 3076
  309.8 15.0 %all-to-all-start = ((bf16[8,2,2048]{2,1,0:T(2,128)(2,1)}), bf16[8,2,2048]{2,1,0:T(2,128)(2,1)S(1)}, u32[]{:S(2)}, u32[]{:S(2)}) async-start(bf16[8,2,2048]{2,1,0:T(2,128)(2,1)} %reshape.81), calls=%async_computation | async-start | bytes 131072 | tf_op jit(solution)/shard_map/all_to_all | solution.py:110
  327.5 52.6 %copy-start.3 = (f32[8,10752]{1,0:T(8,128)S(1)}, f32[8,10752]{1,0:T(8,128)}, u32[]{:S(2)}) copy-start(f32[8,10752]{1,0:T(8,128)} %param.14) | copy-start | bytes 1032196
  327.5 52.6 %copy-start.7 = (f32[8,10752]{1,0:T(8,128)S(1)}, f32[8,10752]{1,0:T(8,128)}, u32[]{:S(2)}) copy-start(f32[8,10752]{1,0:T(8,128)} %get-tuple-element.35) | copy-start | bytes 1032196
  341.4 29.5 %copy-start.9 = (f32[8,10752]{1,0:T(8,128)S(1)}, f32[8,10752]{1,0:T(8,128)}, u32[]{:S(2)}) copy-start(f32[8,10752]{1,0:T(8,128)} %param.11) | copy-start | bytes 1032196
  342.1 10.2 %all-to-all-start.1 = ((bf16[2,128,2,64]{1,0,2,3:T(2,128)(2,1)}), bf16[2,128,2,64]{1,0,2,3:T(2,128)(2,1)S(1)}, u32[]{:S(2)}, u32[]{:S(2)}) async-start(bf16[2,128,2,64]{1,0,2,3:T(2,128)(2,1)} %copy.33), calls=%async_computation.1 | async-start | bytes 131072 | tf_op jit(solution)/shard_map/all_to_all | solution.py:115
  372.2 6.2 %collective-permute-start.4 = (bf16[1,10752]{1,0:T(2,128)(2,1)S(1)}, bf16[1,10752]{1,0:T(2,128)(2,1)S(1)}, u32[]{:S(2)}, u32[]{:S(2)}) collective-permute-start(bf16[1,10752]{1,0:T(2,128)(2,1)S(1)} %slice.278), channel_id=1, source_target_pairs={{4,0},{8,4},{12,8},{16,12},{20,16},{24,20},{28,24},{5,1},{9,5},{13... | collective-permute-start | bytes 64520 | tf_op jit(solution)/shard_map/ppermute | solution.py:18
  373.5 6.5 %collective-permute-start.6 = (bf16[1,10752]{1,0:T(2,128)(2,1)S(1)}, bf16[1,10752]{1,0:T(2,128)(2,1)S(1)}, u32[]{:S(2)}, u32[]{:S(2)}) collective-permute-start(bf16[1,10752]{1,0:T(2,128)(2,1)S(1)} %slice.276), channel_id=1, source_target_pairs={{4,0},{8,4},{12,8},{16,12},{20,16},{24,20},{28,24},{5,1},{9,5},{13... | collective-permute-start | bytes 64520 | tf_op jit(solution)/shard_map/ppermute | solution.py:18
  382.6 7.5 %collective-permute-start.5 = (bf16[1,10752]{1,0:T(2,128)(2,1)S(1)}, bf16[1,10752]{1,0:T(2,128)(2,1)S(1)}, u32[]{:S(2)}, u32[]{:S(2)}) collective-permute-start(bf16[1,10752]{1,0:T(2,128)(2,1)S(1)} %slice.277), channel_id=1, source_target_pairs={{0,4},{4,8},{8,12},{12,16},{16,20},{20,24},{24,28},{1,5},{5,9},{9,... | collective-permute-start | bytes 64520 | tf_op jit(solution)/shard_map/ppermute | solution.py:18
  387.5 5.0 %collective-permute-start.7 = (bf16[1,10752]{1,0:T(2,128)(2,1)S(1)}, bf16[1,10752]{1,0:T(2,128)(2,1)S(1)}, u32[]{:S(2)}, u32[]{:S(2)}) collective-permute-start(bf16[1,10752]{1,0:T(2,128)(2,1)S(1)} %slice.275), channel_id=1, source_target_pairs={{0,4},{4,8},{8,12},{12,16},{16,20},{20,24},{24,28},{1,5},{5,9},{9,... | collective-permute-start | bytes 64520 | tf_op jit(solution)/shard_map/ppermute | solution.py:18
  425.5 51.1 %copy-start.10 = (f32[1,8,10752]{2,1,0:T(8,128)S(1)}, f32[1,8,10752]{2,1,0:T(8,128)}, u32[]{:S(2)}) copy-start(f32[1,8,10752]{2,1,0:T(8,128)} %get-tuple-element.4) | copy-start | bytes 1032196
  427.6 53.7 %copy-start.4 = (f32[8,10752]{1,0:T(8,128)S(1)}, f32[8,10752]{1,0:T(8,128)}, u32[]{:S(2)}) copy-start(f32[8,10752]{1,0:T(8,128)} %param.14) | copy-start | bytes 1032196
  427.7 53.7 %copy-start.6 = (f32[8,10752]{1,0:T(8,128)S(1)}, f32[8,10752]{1,0:T(8,128)}, u32[]{:S(2)}) copy-start(f32[8,10752]{1,0:T(8,128)} %copy-done.5) | copy-start | bytes 1032196
  427.7 53.7 %copy-start.8 = (f32[8,10752]{1,0:T(8,128)S(1)}, f32[8,10752]{1,0:T(8,128)}, u32[]{:S(2)}) copy-start(f32[8,10752]{1,0:T(8,128)} %get-tuple-element.35) | copy-start | bytes 1032196
  475.4 5.9 %collective-permute-start.8 = (bf16[1,10752]{1,0:T(2,128)(2,1)S(1)}, bf16[1,10752]{1,0:T(2,128)(2,1)S(1)}, u32[]{:S(2)}, u32[]{:S(2)}) collective-permute-start(bf16[1,10752]{1,0:T(2,128)(2,1)S(1)} %slice.274), channel_id=1, source_target_pairs={{4,0},{8,4},{12,8},{16,12},{20,16},{24,20},{28,24},{5,1},{9,5},{13... | collective-permute-start | bytes 64520 | tf_op jit(solution)/shard_map/ppermute | solution.py:18
  482.8 4.9 collective-permute-start.9
